TPU v7x, 512 devices: a whole 4x8x8 slice. The times are simulated.
512 devices in a mesh: prompt: 8 (over y), resp: 64 (over z, x, core).
Axes of the slice: x: 4, y: 8, z: 8, core: 2. Of those that a mesh axis runs over, the one named last changes fastest.
Arguments:
- queries: bfloat16 [8, 64, 256, 2048], P('prompt', 'resp')
- resp_kv: bfloat16 [8, 64, 256, 1024], P('prompt', 'resp')
- out_grad: bfloat16 [8, 64, 256, 2048], P('prompt', 'resp'), may hold values from -6 to 6
- prompt_kv: bfloat16 [64, 128, 1024], P('resp', 'prompt'), may hold values from -6 to 6
- prompt_of: int32 [64], replicated, may hold values from 0 to 63, as said below
- lengths: int32 [8, 64], P('prompt', 'resp'), may hold values from 1 to 2
Outputs:
- query_grad: bfloat16 [8, 64, 256, 2048], P('prompt', 'resp')
- resp_kv_grad: bfloat16 [8, 64, 256, 1024], P('prompt', 'resp')
- prompt_kv_grad: float32 [64, 128, 1024], P('resp', 'prompt')
Inputs may be any that keep to these rules, and one draw needn't show every extreme that they name: The cyclic distance between b and prompt_of[b] (mod 64) is at most 3; it is 3 on both sides for some b.
All inputs are finite; a program needn't handle non-finite values.
Results may differ from a plain program's by a relative error of at most 0.024.
Values may be sent and summed in bfloat16 or wider, within the bound.
A program may use at most 64 MiB of HBM per device.

v0:
```python
import jax
import jax.numpy as jnp
from jax import lax
from jax.sharding import PartitionSpec as P

QH = 16
KVH = 4
HD = 128
BLOCK = 128
REACH = 3
masked_value = -1e30


def from_behind(value, axis, steps):
    count = lax.axis_size(axis)
    pairs = [(source, (source + steps) % count) for source in range(count)]
    return lax.ppermute(value, axis, pairs)


def shards(queries, resp_kv, out_grad, prompt_kv, prompt_of, lengths):
    groups = QH // KVH
    softmax_scale = HD ** (-0.5)
    key_width = KVH * HD
    column = lax.axis_index("resp")
    group_size = lax.axis_size("resp")
    wanted = prompt_of[column]
    offset = (column - wanted + group_size + REACH) % group_size - REACH
    own_rows = prompt_kv[0]
    full_rows = lax.all_gather(own_rows, "prompt", axis=0, tiled=True)
    fetched = jnp.where(offset == 0, full_rows, jnp.zeros_like(full_rows))
    for stride in range(1, REACH + 1):
        for signed in (stride, -stride):
            arrived = from_behind(full_rows, "resp", signed)
            fetched = jnp.where(offset == signed, arrived, fetched)
    query_rows = queries[0, 0]
    resp_rows = resp_kv[0, 0]
    grad_rows = out_grad[0, 0]
    resp_len = query_rows.shape[0]
    row_index = jnp.arange(resp_len, dtype=jnp.int32)
    live_rows = row_index < lengths[0, 0] * BLOCK
    masked_grad = jnp.where(live_rows[:, None], grad_rows, jnp.zeros_like(grad_rows))
    causal = row_index[None, :] <= row_index[:, None]
    query_parts = []
    resp_key_parts = []
    resp_value_parts = []
    prompt_key_parts = []
    prompt_value_parts = []
    for head_index in range(KVH):
        query_slice = slice(head_index * groups * HD, (head_index + 1) * groups * HD)
        key_slice = slice(head_index * HD, (head_index + 1) * HD)
        value_slice = slice(key_width + head_index * HD, key_width + (head_index + 1) * HD)
        query_head_block = query_rows[:, query_slice].reshape(resp_len, groups, HD)
        head_gradient = masked_grad[:, query_slice].reshape(resp_len, groups, HD)
        prompt_key_block = fetched[:, key_slice]
        prompt_value_block = fetched[:, value_slice]
        response_key_block = resp_rows[:, key_slice]
        response_value_block = resp_rows[:, value_slice]
        score_resp = (
            jnp.einsum(
                "xjc,bc->jxb",
                query_head_block,
                response_key_block,
                preferred_element_type=jnp.float32,
            )
            * softmax_scale
        )
        score_resp = jnp.where(causal[None], score_resp, masked_value)
        score_prompt = (
            jnp.einsum(
                "xjc,bc->jxb",
                query_head_block,
                prompt_key_block,
                preferred_element_type=jnp.float32,
            )
            * softmax_scale
        )
        top_score = jnp.maximum(
            jnp.max(score_prompt, axis=-1, keepdims=True),
            jnp.max(score_resp, axis=-1, keepdims=True),
        )
        exp_prompt = jnp.exp(score_prompt - top_score)
        exp_resp = jnp.exp(score_resp - top_score)
        total_mass = jnp.sum(exp_prompt, axis=-1, keepdims=True) + jnp.sum(
            exp_resp, axis=-1, keepdims=True
        )
        prob_prompt = exp_prompt / total_mass
        prob_resp = exp_resp / total_mass
        prompt_round_block = prob_prompt.astype(jnp.bfloat16)
        response_round_block = prob_resp.astype(jnp.bfloat16)
        head_out = jnp.einsum(
            "czu,uk->zck",
            prompt_round_block,
            prompt_value_block,
            preferred_element_type=jnp.float32,
        )
        head_out = head_out + jnp.einsum(
            "czu,uk->zck",
            response_round_block,
            response_value_block,
            preferred_element_type=jnp.float32,
        )
        head_out = head_out.astype(jnp.bfloat16)
        row_delta = jnp.sum(
            head_gradient.astype(jnp.float32) * head_out.astype(jnp.float32), axis=-1
        )
        row_delta = jnp.transpose(row_delta, (1, 0))[..., None]
        back_prompt = jnp.einsum(
            "xjc,bc->jxb", head_gradient, prompt_value_block, preferred_element_type=jnp.float32
        )
        back_resp = jnp.einsum(
            "xjc,bc->jxb", head_gradient, response_value_block, preferred_element_type=jnp.float32
        )
        prompt_score_gradient = (prob_prompt * (back_prompt - row_delta)).astype(jnp.bfloat16)
        response_score_gradient = (prob_resp * (back_resp - row_delta)).astype(jnp.bfloat16)
        query_head_grad = jnp.einsum(
            "czu,uk->zck",
            prompt_score_gradient,
            prompt_key_block,
            preferred_element_type=jnp.float32,
        )
        query_head_grad = query_head_grad + jnp.einsum(
            "czu,uk->zck",
            response_score_gradient,
            response_key_block,
            preferred_element_type=jnp.float32,
        )
        query_parts.append(
            (query_head_grad * softmax_scale).astype(jnp.bfloat16).reshape(resp_len, groups * HD)
        )
        prompt_key_parts.append(
            jnp.einsum(
                "lpb,ply->by",
                prompt_score_gradient,
                query_head_block,
                preferred_element_type=jnp.float32,
            )
            * softmax_scale
        )
        prompt_value_parts.append(
            jnp.einsum(
                "lpb,ply->by", prompt_round_block, head_gradient, preferred_element_type=jnp.float32
            )
        )
        resp_key_parts.append(
            jnp.einsum(
                "lpb,ply->by",
                response_score_gradient,
                query_head_block,
                preferred_element_type=jnp.float32,
            )
            * softmax_scale
        )
        resp_value_parts.append(
            jnp.einsum(
                "lpb,ply->by",
                response_round_block,
                head_gradient,
                preferred_element_type=jnp.float32,
            )
        )
    query_grad = jnp.concatenate(query_parts, axis=1)
    resp_grad = jnp.concatenate(resp_key_parts + resp_value_parts, axis=1).astype(jnp.bfloat16)
    prompt_partial = jnp.concatenate(prompt_key_parts + prompt_value_parts, axis=1)
    rows_sum = lax.psum_scatter(prompt_partial, "prompt", scatter_dimension=0, tiled=True)
    collected = jnp.where(wanted == column, rows_sum, jnp.zeros_like(rows_sum))
    for stride in range(1, REACH + 1):
        for signed in (stride, -stride):
            arrived = from_behind(rows_sum.astype(jnp.bfloat16), "resp", -signed).astype(
                rows_sum.dtype
            )
            source = (column + signed + group_size) % group_size
            collected = collected + jnp.where(
                prompt_of[source] == column, arrived, jnp.zeros_like(arrived)
            )
    return (query_grad[None, None], resp_grad[None, None], collected[None])


def solution(mesh):
    return jax.shard_map(
        shards,
        mesh=mesh,
        in_specs=(
            P("prompt", "resp", None, None),
            P("prompt", "resp", None, None),
            P("prompt", "resp", None, None),
            P("resp", "prompt", None),
            P(),
            P("prompt", "resp"),
        ),
        out_specs=(
            P("prompt", "resp", None, None),
            P("prompt", "resp", None, None),
            P("resp", "prompt", None),
        ),
        check_vma=False,
    )
```

profile of v0, /device:TPU:199, one launch (start us, length us, event | category | flops | bytes accessed | tf_op | source)
XLA Modules:
  0.0 191.8 jit_solution(11302706265438290318)
XLA Ops:
  7.2 22.3 %all-gather = bf16[1,128,1024]{2,1,0:T(8,128)(2,1)} all-gather(bf16[1,16,1024]{2,1,0:T(8,128)(2,1)} %param.9), channel_id=2, replica_groups=mesh['prompt'=8,'resp'=64] {'prompt'}, dimensions={1}, use_global_device_ids=true | all-gather | bytes 294912 | tf_op jit(solution)/shard_map/all_gather | solution.py:29
  29.5 12.1 %collective-permute-start.5 = (bf16[128,1024]{1,0:T(8,128)(2,1)}, bf16[128,1024]{1,0:T(8,128)(2,1)}, u32[]{:S(2)}, u32[]{:S(2)}) collective-permute-start(bf16[128,1024]{1,0:T(8,128)(2,1)} %bitcast.1), channel_id=1, source_target_pairs={{0,1},{1,2},{2,3},{3,4},{4,5},{5,6},{6,7},{7,8},{8,9},{9,10},{10,1... | collective-permute-start | bytes 786440 | tf_op jit(solution)/shard_map/ppermute | solution.py:17
  41.6 1.9 %collective-permute-start.4 = (bf16[128,1024]{1,0:T(8,128)(2,1)}, bf16[128,1024]{1,0:T(8,128)(2,1)}, u32[]{:S(2)}, u32[]{:S(2)}) collective-permute-start(bf16[128,1024]{1,0:T(8,128)(2,1)} %bitcast.1), channel_id=1, source_target_pairs={{0,63},{1,0},{2,1},{3,2},{4,3},{5,4},{6,5},{7,6},{8,7},{9,8},{10,9... | collective-permute-start | bytes 786440 | tf_op jit(solution)/shard_map/ppermute | solution.py:17
  43.5 3.1 %collective-permute-start.3 = (bf16[128,1024]{1,0:T(8,128)(2,1)}, bf16[128,1024]{1,0:T(8,128)(2,1)}, u32[]{:S(2)}, u32[]{:S(2)}) collective-permute-start(bf16[128,1024]{1,0:T(8,128)(2,1)} %bitcast.1), channel_id=1, source_target_pairs={{0,2},{1,3},{2,4},{3,5},{4,6},{5,7},{6,8},{7,9},{8,10},{9,11},{10,... | collective-permute-start | bytes 786440 | tf_op jit(solution)/shard_map/ppermute | solution.py:17
  46.7 2.2 %collective-permute-start.2 = (bf16[128,1024]{1,0:T(8,128)(2,1)}, bf16[128,1024]{1,0:T(8,128)(2,1)}, u32[]{:S(2)}, u32[]{:S(2)}) collective-permute-start(bf16[128,1024]{1,0:T(8,128)(2,1)} %bitcast.1), channel_id=1, source_target_pairs={{0,62},{1,63},{2,0},{3,1},{4,2},{5,3},{6,4},{7,5},{8,6},{9,7},{10,... | collective-permute-start | bytes 786440 | tf_op jit(solution)/shard_map/ppermute | solution.py:17
  48.8 7.0 %collective-permute-start.1 = (bf16[128,1024]{1,0:T(8,128)(2,1)}, bf16[128,1024]{1,0:T(8,128)(2,1)}, u32[]{:S(2)}, u32[]{:S(2)}) collective-permute-start(bf16[128,1024]{1,0:T(8,128)(2,1)} %bitcast.1), channel_id=1, source_target_pairs={{0,3},{1,4},{2,5},{3,6},{4,7},{5,8},{6,9},{7,10},{8,11},{9,12},{10... | collective-permute-start | bytes 786440 | tf_op jit(solution)/shard_map/ppermute | solution.py:17
  56.6 1.5 copy.167
  58.1 0.9 fusion.140
  58.9 1.6 copy.170
  60.6 1.0 fusion.141
  61.6 1.1 fusion.144
  62.8 1.2 fusion.150
  64.0 0.7 fusion.142
  66.1 1.3 fusion.146
  67.4 2.1 %collective-permute-start = (bf16[128,1024]{1,0:T(8,128)(2,1)}, bf16[128,1024]{1,0:T(8,128)(2,1)}, u32[]{:S(2)}, u32[]{:S(2)}) collective-permute-start(bf16[128,1024]{1,0:T(8,128)(2,1)} %bitcast.1), channel_id=1, source_target_pairs={{0,61},{1,62},{2,63},{3,0},{4,1},{5,2},{6,3},{7,4},{8,5},{9,6},{10... | collective-permute-start | bytes 786440 | tf_op jit(solution)/shard_map/ppermute | solution.py:17
  73.1 1.3 fusion.148
  74.5 6.2 %collective-permute-done = bf16[128,1024]{1,0:T(8,128)(2,1)} collective-permute-done((bf16[128,1024]{1,0:T(8,128)(2,1)}, bf16[128,1024]{1,0:T(8,128)(2,1)}, u32[]{:S(2)}, u32[]{:S(2)}) %collective-permute-start) | collective-permute-done | bytes 262176 | tf_op jit(solution)/shard_map/ppermute | solution.py:17
  80.7 1.0 select_select_fusion
  82.2 0.5 copy-done
  83.6 0.7 copy-done.9
  85.2 0.3 fusion.16
  86.5 0.5 copy-done.19
  87.8 0.9 fusion.89
  89.7 0.5 copy-done.15
  90.5 0.3 fusion.17
  91.8 0.5 copy-done.17
  93.4 0.8 fusion.107
  94.2 1.0 fusion.50
  95.8 0.9 fusion.91
  96.7 1.0 fusion.48
  97.7 0.8 fusion.105
  98.5 1.0 fusion.46
  99.5 0.8 fusion.103
  100.3 1.0 fusion.44
  101.3 0.9 fusion.101
  102.1 0.9 fusion.99
  103.0 0.9 fusion.98
  103.9 0.9 fusion.97
  104.8 0.9 fusion.96
  105.7 2.1 %copy.327 = f32[128,1024]{1,0:T(8,128)} copy(f32[128,1024]{0,1:T(8,128)} %fusion.96) | data formatting | bytes 1048576
  107.8 0.9 fusion.93
  108.7 1.9 copy.224
  110.6 0.9 copy.221
  111.5 0.8 copy.223
  112.3 0.9 copy.222
  113.2 0.9 fusion.95
  114.2 0.9 fusion.87
  115.1 0.9 fusion.85
  116.1 1.1 maximum_bitcast_fusion
  117.2 24.7 %reduce-scatter.4.cloned.1.call-done = f32[16,1024]{1,0:T(8,128)} async-done(((f32[128,1024]{1,0:T(8,128)}), f32[16,1024]{1,0:T(8,128)}) %reduce-scatter.4.cloned.1.call-update) | async-done | bytes 65552
  141.9 1.0 copy.328
  142.9 10.9 %collective-permute-start.11 = (bf16[16,1024]{0,1:T(8,128)(2,1)S(1)}, bf16[16,1024]{0,1:T(8,128)(2,1)S(1)}, u32[]{:S(2)}, u32[]{:S(2)}) collective-permute-start(bf16[16,1024]{0,1:T(8,128)(2,1)S(1)} %convert_element_type.162), channel_id=1, source_target_pairs={{0,3},{1,4},{2,5},{3,6},{4,7},{5,8},{6,9},{7,10},{8,11},{9,12},{10... | collective-permute-start | bytes 98312 | tf_op jit(solution)/shard_map/ppermute | solution.py:17
  153.9 0.3 fusion.83
  154.2 1.9 %collective-permute-start.10 = (bf16[16,1024]{0,1:T(8,128)(2,1)S(1)}, bf16[16,1024]{0,1:T(8,128)(2,1)S(1)}, u32[]{:S(2)}, u32[]{:S(2)}) collective-permute-start(bf16[16,1024]{0,1:T(8,128)(2,1)S(1)} %convert_element_type.162), channel_id=1, source_target_pairs={{0,61},{1,62},{2,63},{3,0},{4,1},{5,2},{6,3},{7,4},{8,5},{9,6},{10... | collective-permute-start | bytes 98312 | tf_op jit(solution)/shard_map/ppermute | solution.py:17
  156.1 3.7 %collective-permute-start.9 = (bf16[16,1024]{0,1:T(8,128)(2,1)S(1)}, bf16[16,1024]{0,1:T(8,128)(2,1)S(1)}, u32[]{:S(2)}, u32[]{:S(2)}) collective-permute-start(bf16[16,1024]{0,1:T(8,128)(2,1)S(1)} %convert_element_type.162), channel_id=1, source_target_pairs={{0,2},{1,3},{2,4},{3,5},{4,6},{5,7},{6,8},{7,9},{8,10},{9,11},{10,... | collective-permute-start | bytes 98312 | tf_op jit(solution)/shard_map/ppermute | solution.py:17
  159.8 1.9 %collective-permute-start.8 = (bf16[16,1024]{0,1:T(8,128)(2,1)S(1)}, bf16[16,1024]{0,1:T(8,128)(2,1)S(1)}, u32[]{:S(2)}, u32[]{:S(2)}) collective-permute-start(bf16[16,1024]{0,1:T(8,128)(2,1)S(1)} %convert_element_type.162), channel_id=1, source_target_pairs={{0,62},{1,63},{2,0},{3,1},{4,2},{5,3},{6,4},{7,5},{8,6},{9,7},{10,... | collective-permute-start | bytes 98312 | tf_op jit(solution)/shard_map/ppermute | solution.py:17
  161.8 9.9 %collective-permute-start.7 = (bf16[16,1024]{0,1:T(8,128)(2,1)S(1)}, bf16[16,1024]{0,1:T(8,128)(2,1)S(1)}, u32[]{:S(2)}, u32[]{:S(2)}) collective-permute-start(bf16[16,1024]{0,1:T(8,128)(2,1)S(1)} %convert_element_type.162), channel_id=1, source_target_pairs={{0,1},{1,2},{2,3},{3,4},{4,5},{5,6},{6,7},{7,8},{8,9},{9,10},{10,1... | collective-permute-start | bytes 98312 | tf_op jit(solution)/shard_map/ppermute | solution.py:17
  171.6 1.9 %collective-permute-start.6 = (bf16[16,1024]{0,1:T(8,128)(2,1)S(1)}, bf16[16,1024]{0,1:T(8,128)(2,1)}, u32[]{:S(2)}, u32[]{:S(2)}) collective-permute-start(bf16[16,1024]{0,1:T(8,128)(2,1)S(1)} %convert_element_type.162), channel_id=1, source_target_pairs={{0,63},{1,0},{2,1},{3,2},{4,3},{5,4},{6,5},{7,6},{8,7},{9,8},{10,9... | collective-permute-start | bytes 98312 | tf_op jit(solution)/shard_map/ppermute | solution.py:17
  173.6 0.3 fusion.81
  173.9 1.0 copy.241
  174.9 0.7 copy-done.26
  175.6 7.1 %collective-permute-done.6 = bf16[16,1024]{0,1:T(8,128)(2,1)} collective-permute-done((bf16[16,1024]{0,1:T(8,128)(2,1)S(1)}, bf16[16,1024]{0,1:T(8,128)(2,1)}, u32[]{:S(2)}, u32[]{:S(2)}) %collective-permute-start.6) | collective-permute-done | bytes 32800 | tf_op jit(solution)/shard_map/ppermute | solution.py:17
  182.8 1.4 add_bitcast_fusion
  184.1 0.8 copy.242
  (108 shorter events, 8.0 us)
Async XLA Ops:
  7.2 134.7 %reduce-scatter.4.cloned.1.call-start = ((), (), s32[]{:S(2)}) async-start(), calls=%async_computation.1 | async-start | bytes 589824
  29.5 37.9 %collective-permute-start.5 = (bf16[128,1024]{1,0:T(8,128)(2,1)}, bf16[128,1024]{1,0:T(8,128)(2,1)}, u32[]{:S(2)}, u32[]{:S(2)}) collective-permute-start(bf16[128,1024]{1,0:T(8,128)(2,1)} %bitcast.1), channel_id=1, source_target_pairs={{0,1},{1,2},{2,3},{3,4},{4,5},{5,6},{6,7},{7,8},{8,9},{9,10},{10,1... | collective-permute-start | bytes 786440 | tf_op jit(solution)/shard_map/ppermute | solution.py:17
  41.6 32.8 %collective-permute-start.4 = (bf16[128,1024]{1,0:T(8,128)(2,1)}, bf16[128,1024]{1,0:T(8,128)(2,1)}, u32[]{:S(2)}, u32[]{:S(2)}) collective-permute-start(bf16[128,1024]{1,0:T(8,128)(2,1)} %bitcast.1), channel_id=1, source_target_pairs={{0,63},{1,0},{2,1},{3,2},{4,3},{5,4},{6,5},{7,6},{8,7},{9,8},{10,9... | collective-permute-start | bytes 786440 | tf_op jit(solution)/shard_map/ppermute | solution.py:17
  43.5 30.9 %collective-permute-start.3 = (bf16[128,1024]{1,0:T(8,128)(2,1)}, bf16[128,1024]{1,0:T(8,128)(2,1)}, u32[]{:S(2)}, u32[]{:S(2)}) collective-permute-start(bf16[128,1024]{1,0:T(8,128)(2,1)} %bitcast.1), channel_id=1, source_target_pairs={{0,2},{1,3},{2,4},{3,5},{4,6},{5,7},{6,8},{7,9},{8,10},{9,11},{10,... | collective-permute-start | bytes 786440 | tf_op jit(solution)/shard_map/ppermute | solution.py:17
  46.7 27.8 %collective-permute-start.2 = (bf16[128,1024]{1,0:T(8,128)(2,1)}, bf16[128,1024]{1,0:T(8,128)(2,1)}, u32[]{:S(2)}, u32[]{:S(2)}) collective-permute-start(bf16[128,1024]{1,0:T(8,128)(2,1)} %bitcast.1), channel_id=1, source_target_pairs={{0,62},{1,63},{2,0},{3,1},{4,2},{5,3},{6,4},{7,5},{8,6},{9,7},{10,... | collective-permute-start | bytes 786440 | tf_op jit(solution)/shard_map/ppermute | solution.py:17
  48.8 25.6 %collective-permute-start.1 = (bf16[128,1024]{1,0:T(8,128)(2,1)}, bf16[128,1024]{1,0:T(8,128)(2,1)}, u32[]{:S(2)}, u32[]{:S(2)}) collective-permute-start(bf16[128,1024]{1,0:T(8,128)(2,1)} %bitcast.1), channel_id=1, source_target_pairs={{0,3},{1,4},{2,5},{3,6},{4,7},{5,8},{6,9},{7,10},{8,11},{9,12},{10... | collective-permute-start | bytes 786440 | tf_op jit(solution)/shard_map/ppermute | solution.py:17
  58.9 3.8 %copy-start.3 = (bf16[256,512]{0,1:T(8,128)(2,1)}, bf16[256,512]{0,1:T(8,128)(2,1)S(1)}, u32[]{:S(2)}) copy-start(bf16[256,512]{0,1:T(8,128)(2,1)S(1)} %get-tuple-element.12) | copy-start | bytes 786436
  62.8 1.2 copy-start.27
  67.4 13.3 %collective-permute-start = (bf16[128,1024]{1,0:T(8,128)(2,1)}, bf16[128,1024]{1,0:T(8,128)(2,1)}, u32[]{:S(2)}, u32[]{:S(2)}) collective-permute-start(bf16[128,1024]{1,0:T(8,128)(2,1)} %bitcast.1), channel_id=1, source_target_pairs={{0,61},{1,62},{2,63},{3,0},{4,1},{5,2},{6,3},{7,4},{8,5},{9,6},{10... | collective-permute-start | bytes 786440 | tf_op jit(solution)/shard_map/ppermute | solution.py:17
  74.4 7.6 %copy-start.4 = (bf16[256,512]{0,1:T(8,128)(2,1)S(1)}, bf16[256,512]{0,1:T(8,128)(2,1)}, u32[]{:S(2)}) copy-start(bf16[256,512]{0,1:T(8,128)(2,1)} %copy-done.3) | copy-start | bytes 786436
  81.7 1.0 copy-start
  81.7 1.2 copy-start.2
  83.3 1.0 copy-start.9
  83.4 1.2 copy-start.13
  84.4 0.8 copy-start.5
  85.5 7.6 %copy-start.7 = (bf16[4,256,256]{1,2,0:T(8,128)(2,1)}, bf16[4,256,256]{1,2,0:T(8,128)(2,1)S(1)}, u32[]{:S(2)}) copy-start(bf16[4,256,256]{1,2,0:T(8,128)(2,1)S(1)} %fusion.16) | copy-start | bytes 1572868
  86.0 1.0 copy-start.19
  89.3 1.0 copy-start.15
  91.4 1.0 copy-start.17
  105.7 2.1 %copy-start.1 = (bf16[256,512]{0,1:T(8,128)(2,1)S(1)}, bf16[256,512]{0,1:T(8,128)(2,1)}, u32[]{:S(2)}) copy-start(bf16[256,512]{0,1:T(8,128)(2,1)} %get-tuple-element.14) | copy-start | bytes 786436
  107.7 2.9 %copy-start.10 = (bf16[256,4,128]{0,2,1:T(8,128)(2,1)S(1)}, bf16[256,4,128]{0,2,1:T(8,128)(2,1)}, u32[]{:S(2)}) copy-start(bf16[256,4,128]{0,2,1:T(8,128)(2,1)} %fusion.50) | copy-start | bytes 786436
  107.8 4.6 %copy-start.11 = (bf16[256,4,128]{0,2,1:T(8,128)(2,1)S(1)}, bf16[256,4,128]{0,2,1:T(8,128)(2,1)}, u32[]{:S(2)}) copy-start(bf16[256,4,128]{0,2,1:T(8,128)(2,1)} %fusion.48) | copy-start | bytes 786436
  108.7 2.8 %copy-start.12 = (bf16[256,4,128]{0,2,1:T(8,128)(2,1)S(1)}, bf16[256,4,128]{0,2,1:T(8,128)(2,1)}, u32[]{:S(2)}) copy-start(bf16[256,4,128]{0,2,1:T(8,128)(2,1)} %fusion.46) | copy-start | bytes 786436
  108.7 4.5 %copy-start.8 = (bf16[4,256,256]{1,2,0:T(8,128)(2,1)S(1)}, bf16[4,256,256]{1,2,0:T(8,128)(2,1)}, u32[]{:S(2)}) copy-start(bf16[4,256,256]{1,2,0:T(8,128)(2,1)} %copy-done.7) | copy-start | bytes 1572868
  111.5 2.7 %copy-start.20 = (bf16[256,512]{0,1:T(8,128)(2,1)S(1)}, bf16[256,512]{0,1:T(8,128)(2,1)}, u32[]{:S(2)}) copy-start(bf16[256,512]{0,1:T(8,128)(2,1)} %get-tuple-element.16) | copy-start | bytes 786436
  112.3 2.8 %copy-start.18 = (bf16[256,512]{0,1:T(8,128)(2,1)S(1)}, bf16[256,512]{0,1:T(8,128)(2,1)}, u32[]{:S(2)}) copy-start(bf16[256,512]{0,1:T(8,128)(2,1)} %get-tuple-element.19) | copy-start | bytes 786436
  114.1 1.9 copy-start.21
  114.1 1.9 copy-start.22
  114.1 1.9 copy-start.23
  114.1 1.9 copy-start.24
  116.1 37.8 %copy-start.25 = (bf16[1,1,256,1024]{2,3,1,0:T(8,128)(2,1)S(1)}, bf16[1,1,256,1024]{2,3,1,0:T(8,128)(2,1)}, u32[]{:S(2)}) copy-start(bf16[1,1,256,1024]{2,3,1,0:T(8,128)(2,1)} %fusion.85) | copy-start | bytes 1572868
  117.2 36.7 %copy-start.16 = (bf16[256,512]{0,1:T(8,128)(2,1)S(1)}, bf16[256,512]{0,1:T(8,128)(2,1)}, u32[]{:S(2)}) copy-start(bf16[256,512]{0,1:T(8,128)(2,1)} %get-tuple-element.18) | copy-start | bytes 786436
  117.2 56.4 %copy-start.6 = (bf16[4,256,256]{1,2,0:T(8,128)(2,1)S(1)}, bf16[4,256,256]{1,2,0:T(8,128)(2,1)}, u32[]{:S(2)}) copy-start(bf16[4,256,256]{1,2,0:T(8,128)(2,1)} %copy-done.5) | copy-start | bytes 1572868
  117.2 56.4 %copy-start.14 = (bf16[256,512]{0,1:T(8,128)(2,1)S(1)}, bf16[256,512]{0,1:T(8,128)(2,1)}, u32[]{:S(2)}) copy-start(bf16[256,512]{0,1:T(8,128)(2,1)} %get-tuple-element.17) | copy-start | bytes 786436
  142.9 28.7 %collective-permute-start.11 = (bf16[16,1024]{0,1:T(8,128)(2,1)S(1)}, bf16[16,1024]{0,1:T(8,128)(2,1)S(1)}, u32[]{:S(2)}, u32[]{:S(2)}) collective-permute-start(bf16[16,1024]{0,1:T(8,128)(2,1)S(1)} %convert_element_type.162), channel_id=1, source_target_pairs={{0,3},{1,4},{2,5},{3,6},{4,7},{5,8},{6,9},{7,10},{8,11},{9,12},{10... | collective-permute-start | bytes 98312 | tf_op jit(solution)/shard_map/ppermute | solution.py:17
  154.2 20.7 %collective-permute-start.10 = (bf16[16,1024]{0,1:T(8,128)(2,1)S(1)}, bf16[16,1024]{0,1:T(8,128)(2,1)S(1)}, u32[]{:S(2)}, u32[]{:S(2)}) collective-permute-start(bf16[16,1024]{0,1:T(8,128)(2,1)S(1)} %convert_element_type.162), channel_id=1, source_target_pairs={{0,61},{1,62},{2,63},{3,0},{4,1},{5,2},{6,3},{7,4},{8,5},{9,6},{10... | collective-permute-start | bytes 98312 | tf_op jit(solution)/shard_map/ppermute | solution.py:17
  156.1 18.8 %collective-permute-start.9 = (bf16[16,1024]{0,1:T(8,128)(2,1)S(1)}, bf16[16,1024]{0,1:T(8,128)(2,1)S(1)}, u32[]{:S(2)}, u32[]{:S(2)}) collective-permute-start(bf16[16,1024]{0,1:T(8,128)(2,1)S(1)} %convert_element_type.162), channel_id=1, source_target_pairs={{0,2},{1,3},{2,4},{3,5},{4,6},{5,7},{6,8},{7,9},{8,10},{9,11},{10,... | collective-permute-start | bytes 98312 | tf_op jit(solution)/shard_map/ppermute | solution.py:17
  159.8 15.1 %collective-permute-start.8 = (bf16[16,1024]{0,1:T(8,128)(2,1)S(1)}, bf16[16,1024]{0,1:T(8,128)(2,1)S(1)}, u32[]{:S(2)}, u32[]{:S(2)}) collective-permute-start(bf16[16,1024]{0,1:T(8,128)(2,1)S(1)} %convert_element_type.162), channel_id=1, source_target_pairs={{0,62},{1,63},{2,0},{3,1},{4,2},{5,3},{6,4},{7,5},{8,6},{9,7},{10,... | collective-permute-start | bytes 98312 | tf_op jit(solution)/shard_map/ppermute | solution.py:17
  161.8 13.2 %collective-permute-start.7 = (bf16[16,1024]{0,1:T(8,128)(2,1)S(1)}, bf16[16,1024]{0,1:T(8,128)(2,1)S(1)}, u32[]{:S(2)}, u32[]{:S(2)}) collective-permute-start(bf16[16,1024]{0,1:T(8,128)(2,1)S(1)} %convert_element_type.162), channel_id=1, source_target_pairs={{0,1},{1,2},{2,3},{3,4},{4,5},{5,6},{6,7},{7,8},{8,9},{9,10},{10,1... | collective-permute-start | bytes 98312 | tf_op jit(solution)/shard_map/ppermute | solution.py:17
  171.6 11.1 %collective-permute-start.6 = (bf16[16,1024]{0,1:T(8,128)(2,1)S(1)}, bf16[16,1024]{0,1:T(8,128)(2,1)}, u32[]{:S(2)}, u32[]{:S(2)}) collective-permute-start(bf16[16,1024]{0,1:T(8,128)(2,1)S(1)} %convert_element_type.162), channel_id=1, source_target_pairs={{0,63},{1,0},{2,1},{3,2},{4,3},{5,4},{6,5},{7,6},{8,7},{9,8},{10,9... | collective-permute-start | bytes 98312 | tf_op jit(solution)/shard_map/ppermute | solution.py:17
  174.9 0.7 copy-start.26
Sparse Core Ops, SparseCore 0:
  107.9 33.9 reduce-scatter.3
where the time goes:
time: 193 us; the launch traced here: 192 us
  starting transfers between devices  58.7 us (30%)
  waiting for transfers between devices  38.1 us (20%)
  matrix products  28.2 us (15%)
  blocking collectives  22.3 us (12%)
  between operations  20.5 us (11%)
  local copies, waits for them, and re-layouts  18.7 us (10%)
  other arithmetic  5.38 us (3%)
    ppermute x12, starting transfers between devices, from_behind(): return lax.ppermute(value, axis, pairs)  58.6 us
    unnamed x2, waiting for transfers between devices  24.7 us
    all_gather x1, blocking collectives, shards(): full_rows = lax.all_gather(own_rows, 'prompt', axis=0, tiled=True)  22.3 us
    ppermute x12, waiting for transfers between devices, from_behind(): return lax.ppermute(value, axis, pairs)  13.4 us
    unnamed x62, local copies, waits for them, and re-layouts  11.7 us
    dot_general x4, matrix products, shards(): jnp.einsum('xjc,bc->jxb', query_head_block, response_key_block, preferred...  4.9 us
    reshape x4, local copies, waits for them, and re-layouts, shards(): (query_head_grad * softmax_scale).astype(jnp.bfloat16)  4.45 us
  transfers between devices with their start and end apart: 13, of which 3 were waited for; matrix products, arithmetic and copies ran while one was open for 11% of the time, Pallas kernels for 0%

commit v1 on v0

--- a/solution.py
+++ b/solution.py
@@ -26,7 +26,10 @@
     wanted = prompt_of[column]
     offset = (column - wanted + group_size + REACH) % group_size - REACH
     own_rows = prompt_kv[0]
-    full_rows = lax.all_gather(own_rows, "prompt", axis=0, tiled=True)
+    size = lax.axis_size("prompt")
+    blocks = jnp.stack([own_rows for _ in range(size)])
+    blocks = lax.all_to_all(blocks, "prompt", split_axis=0, concat_axis=0)
+    full_rows = jnp.concatenate(blocks, axis=0)
     fetched = jnp.where(offset == 0, full_rows, jnp.zeros_like(full_rows))
     for stride in range(1, REACH + 1):
         for signed in (stride, -stride):

time: 193 us -> 173 us (0.90)
  blocking collectives: 22.3 us -> 0 us
  starting transfers between devices: 58.7 us -> 60.9 us
    all_gather x1 -> x0, blocking collectives: 22.3 us -> none  [shards(): full_rows = lax.all_gather(own_rows, 'prompt', axis=0, tiled=True)]
    all_to_all x0 -> x1, starting transfers between devices: none -> 6.82 us  [shards(): blocks = lax.all_to_all(blocks, 'prompt', split_axis=0, concat_axis=0)]
    ppermute x12, starting transfers between devices: 58.6 us -> 54 us  [from_behind(): return lax.ppermute(value, axis, pairs)]
    unnamed x2, waiting for transfers between devices: 24.7 us -> 20.2 us
    all_to_all x0 -> x1, waiting for transfers between devices: none -> 3.73 us  [shards(): blocks = lax.all_to_all(blocks, 'prompt', split_axis=0, concat_axis=0)]
    unnamed x62 -> x68, local copies, waits for them, and re-layouts: 11.7 us -> 10.9 us
  transfers between devices with their start and end apart: 13 -> 14, of which waited for: 3 -> 4; matrix products, arithmetic and copies ran while one was open for 11% -> 11% of each run, Pallas kernels for 0% -> 0%
where the time goes in v1:
time: 173 us; the launch traced here: 172 us
  starting transfers between devices  60.9 us (35%)
  waiting for transfers between devices  37.3 us (22%)
  matrix products  28.2 us (16%)
  between operations  20.7 us (12%)
  local copies, waits for them, and re-layouts  19.5 us (11%)
  other arithmetic  5.46 us (3%)
    ppermute x12, starting transfers between devices, from_behind(): return lax.ppermute(value, axis, pairs)  54 us
    unnamed x2, waiting for transfers between devices  20.2 us
    ppermute x12, waiting for transfers between devices, from_behind(): return lax.ppermute(value, axis, pairs)  13.4 us
    unnamed x68, local copies, waits for them, and re-layouts  10.9 us
    all_to_all x1, starting transfers between devices, shards(): blocks = lax.all_to_all(blocks, 'prompt', split_axis=0, concat_axis=0)  6.82 us
    dot_general x4, matrix products, shards(): jnp.einsum('xjc,bc->jxb', query_head_block, response_key_block, preferred...  4.9 us
    reshape x4, local copies, waits for them, and re-layouts, shards(): (query_head_grad * softmax_scale).astype(jnp.bfloat16)  4.45 us
    dot_general x4, matrix products, shards(): jnp.einsum('czu,uk->zck', prompt_score_gradient, prompt_key_block, prefer...  3.85 us
  transfers between devices with their start and end apart: 14, of which 4 were waited for; matrix products, arithmetic and copies ran while one was open for 11% of the time, Pallas kernels for 0%

profile of v1, /device:TPU:199, one launch (start us, length us, event | category | flops | bytes accessed | tf_op | source)
XLA Modules:
  0.0 172.0 jit_solution(13845226126004527993)
XLA Ops:
  7.2 1.6 stack.3
  8.7 6.8 %all-to-all-start = ((bf16[8,16,1024]{2,1,0:T(8,128)(2,1)}), bf16[8,16,1024]{2,1,0:T(8,128)(2,1)}, u32[]{:S(2)}, u32[]{:S(2)}) async-start(bf16[8,16,1024]{2,1,0:T(8,128)(2,1)} %stack.3), calls=%async_computation | async-start | bytes 524288 | tf_op jit(solution)/shard_map/all_to_all | solution.py:31
  16.4 0.5 copy.167
  16.9 0.9 fusion.140
  17.8 0.5 copy-done.11
  18.3 0.5 copy.170
  19.0 1.1 fusion.144
  20.1 1.0 fusion.141
  21.2 1.2 fusion.150
  22.3 3.7 %all-to-all-done = bf16[8,16,1024]{2,1,0:T(8,128)(2,1)} async-done(((bf16[8,16,1024]{2,1,0:T(8,128)(2,1)}), bf16[8,16,1024]{2,1,0:T(8,128)(2,1)}, u32[]{:S(2)}, u32[]{:S(2)}) %all-to-all-start) | async-done | bytes 262176 | tf_op jit(solution)/shard_map/all_to_all | solution.py:31
  26.0 7.5 %collective-permute-start.5 = (bf16[128,1024]{1,0:T(8,128)(2,1)}, bf16[128,1024]{1,0:T(8,128)(2,1)}, u32[]{:S(2)}, u32[]{:S(2)}) collective-permute-start(bf16[128,1024]{1,0:T(8,128)(2,1)} %bitcast.2), channel_id=1, source_target_pairs={{0,1},{1,2},{2,3},{3,4},{4,5},{5,6},{6,7},{7,8},{8,9},{9,10},{10,1... | collective-permute-start | bytes 786440 | tf_op jit(solution)/shard_map/ppermute | solution.py:17
  33.5 0.7 fusion.142
  35.5 1.3 fusion.146
  36.8 1.9 %collective-permute-start.4 = (bf16[128,1024]{1,0:T(8,128)(2,1)}, bf16[128,1024]{1,0:T(8,128)(2,1)}, u32[]{:S(2)}, u32[]{:S(2)}) collective-permute-start(bf16[128,1024]{1,0:T(8,128)(2,1)} %bitcast.2), channel_id=1, source_target_pairs={{0,63},{1,0},{2,1},{3,2},{4,3},{5,4},{6,5},{7,6},{8,7},{9,8},{10,9... | collective-permute-start | bytes 786440 | tf_op jit(solution)/shard_map/ppermute | solution.py:17
  38.7 3.1 %collective-permute-start.3 = (bf16[128,1024]{1,0:T(8,128)(2,1)}, bf16[128,1024]{1,0:T(8,128)(2,1)}, u32[]{:S(2)}, u32[]{:S(2)}) collective-permute-start(bf16[128,1024]{1,0:T(8,128)(2,1)} %bitcast.2), channel_id=1, source_target_pairs={{0,2},{1,3},{2,4},{3,5},{4,6},{5,7},{6,8},{7,9},{8,10},{9,11},{10,... | collective-permute-start | bytes 786440 | tf_op jit(solution)/shard_map/ppermute | solution.py:17
  41.8 2.2 %collective-permute-start.2 = (bf16[128,1024]{1,0:T(8,128)(2,1)}, bf16[128,1024]{1,0:T(8,128)(2,1)}, u32[]{:S(2)}, u32[]{:S(2)}) collective-permute-start(bf16[128,1024]{1,0:T(8,128)(2,1)} %bitcast.2), channel_id=1, source_target_pairs={{0,62},{1,63},{2,0},{3,1},{4,2},{5,3},{6,4},{7,5},{8,6},{9,7},{10,... | collective-permute-start | bytes 786440 | tf_op jit(solution)/shard_map/ppermute | solution.py:17
  44.0 7.0 %collective-permute-start.1 = (bf16[128,1024]{1,0:T(8,128)(2,1)}, bf16[128,1024]{1,0:T(8,128)(2,1)}, u32[]{:S(2)}, u32[]{:S(2)}) collective-permute-start(bf16[128,1024]{1,0:T(8,128)(2,1)} %bitcast.2), channel_id=1, source_target_pairs={{0,3},{1,4},{2,5},{3,6},{4,7},{5,8},{6,9},{7,10},{8,11},{9,12},{10... | collective-permute-start | bytes 786440 | tf_op jit(solution)/shard_map/ppermute | solution.py:17
  51.0 2.1 %collective-permute-start = (bf16[128,1024]{1,0:T(8,128)(2,1)}, bf16[128,1024]{1,0:T(8,128)(2,1)}, u32[]{:S(2)}, u32[]{:S(2)}) collective-permute-start(bf16[128,1024]{1,0:T(8,128)(2,1)} %bitcast.2), channel_id=1, source_target_pairs={{0,61},{1,62},{2,63},{3,0},{4,1},{5,2},{6,3},{7,4},{8,5},{9,6},{10... | collective-permute-start | bytes 786440 | tf_op jit(solution)/shard_map/ppermute | solution.py:17
  57.0 1.3 fusion.148
  58.4 6.9 %collective-permute-done = bf16[128,1024]{1,0:T(8,128)(2,1)} collective-permute-done((bf16[128,1024]{1,0:T(8,128)(2,1)}, bf16[128,1024]{1,0:T(8,128)(2,1)}, u32[]{:S(2)}, u32[]{:S(2)}) %collective-permute-start) | collective-permute-done | bytes 262176 | tf_op jit(solution)/shard_map/ppermute | solution.py:17
  65.3 1.0 select_select_fusion
  66.8 0.5 copy-done
  68.2 0.7 copy-done.9
  71.1 0.5 copy-done.21
  72.4 0.9 fusion.89
  74.3 0.5 copy-done.17
  76.4 0.5 copy-done.19
  78.0 0.8 fusion.107
  78.8 1.0 fusion.50
  80.3 0.9 fusion.91
  81.3 1.0 fusion.48
  82.3 0.8 fusion.105
  83.1 1.0 fusion.46
  84.1 0.8 fusion.103
  84.9 1.0 fusion.44
  85.9 0.9 fusion.101
  86.7 0.9 fusion.99
  87.6 0.9 fusion.98
  88.5 0.9 fusion.97
  89.4 0.9 fusion.96
  90.2 2.1 %copy.327 = f32[128,1024]{1,0:T(8,128)} copy(f32[128,1024]{0,1:T(8,128)} %fusion.96) | data formatting | bytes 1048576
  92.4 0.9 fusion.93
  93.3 1.9 %copy.224 = bf16[256,512]{1,0:T(8,128)(2,1)} copy(bf16[256,512]{0,1:T(8,128)(2,1)} %bitcast.552) | data formatting | bytes 524288 | tf_op jit(solution)/shard_map/reshape | solution.py:131
  95.2 0.9 copy.221
  96.1 0.8 copy.223
  96.9 0.9 copy.222
  97.8 0.9 fusion.95
  98.7 0.9 fusion.87
  99.7 0.9 fusion.85
  100.7 1.1 maximum_bitcast_fusion
  101.8 20.2 %reduce-scatter.4.cloned.1.call-done = f32[16,1024]{1,0:T(8,128)} async-done(((f32[128,1024]{1,0:T(8,128)}), f32[16,1024]{1,0:T(8,128)}) %reduce-scatter.4.cloned.1.call-update) | async-done | bytes 65552
  121.9 1.0 copy.328
  123.0 10.9 %collective-permute-start.11 = (bf16[16,1024]{0,1:T(8,128)(2,1)S(1)}, bf16[16,1024]{0,1:T(8,128)(2,1)S(1)}, u32[]{:S(2)}, u32[]{:S(2)}) collective-permute-start(bf16[16,1024]{0,1:T(8,128)(2,1)S(1)} %convert_element_type.162), channel_id=1, source_target_pairs={{0,3},{1,4},{2,5},{3,6},{4,7},{5,8},{6,9},{7,10},{8,11},{9,12},{10... | collective-permute-start | bytes 98312 | tf_op jit(solution)/shard_map/ppermute | solution.py:17
  134.3 1.9 %collective-permute-start.10 = (bf16[16,1024]{0,1:T(8,128)(2,1)S(1)}, bf16[16,1024]{0,1:T(8,128)(2,1)S(1)}, u32[]{:S(2)}, u32[]{:S(2)}) collective-permute-start(bf16[16,1024]{0,1:T(8,128)(2,1)S(1)} %convert_element_type.162), channel_id=1, source_target_pairs={{0,61},{1,62},{2,63},{3,0},{4,1},{5,2},{6,3},{7,4},{8,5},{9,6},{10... | collective-permute-start | bytes 98312 | tf_op jit(solution)/shard_map/ppermute | solution.py:17
  136.2 3.7 %collective-permute-start.9 = (bf16[16,1024]{0,1:T(8,128)(2,1)S(1)}, bf16[16,1024]{0,1:T(8,128)(2,1)S(1)}, u32[]{:S(2)}, u32[]{:S(2)}) collective-permute-start(bf16[16,1024]{0,1:T(8,128)(2,1)S(1)} %convert_element_type.162), channel_id=1, source_target_pairs={{0,2},{1,3},{2,4},{3,5},{4,6},{5,7},{6,8},{7,9},{8,10},{9,11},{10,... | collective-permute-start | bytes 98312 | tf_op jit(solution)/shard_map/ppermute | solution.py:17
  139.9 1.9 %collective-permute-start.8 = (bf16[16,1024]{0,1:T(8,128)(2,1)S(1)}, bf16[16,1024]{0,1:T(8,128)(2,1)S(1)}, u32[]{:S(2)}, u32[]{:S(2)}) collective-permute-start(bf16[16,1024]{0,1:T(8,128)(2,1)S(1)} %convert_element_type.162), channel_id=1, source_target_pairs={{0,62},{1,63},{2,0},{3,1},{4,2},{5,3},{6,4},{7,5},{8,6},{9,7},{10,... | collective-permute-start | bytes 98312 | tf_op jit(solution)/shard_map/ppermute | solution.py:17
  141.9 9.9 %collective-permute-start.7 = (bf16[16,1024]{0,1:T(8,128)(2,1)S(1)}, bf16[16,1024]{0,1:T(8,128)(2,1)S(1)}, u32[]{:S(2)}, u32[]{:S(2)}) collective-permute-start(bf16[16,1024]{0,1:T(8,128)(2,1)S(1)} %convert_element_type.162), channel_id=1, source_target_pairs={{0,1},{1,2},{2,3},{3,4},{4,5},{5,6},{6,7},{7,8},{8,9},{9,10},{10,1... | collective-permute-start | bytes 98312 | tf_op jit(solution)/shard_map/ppermute | solution.py:17
  151.8 1.9 %collective-permute-start.6 = (bf16[16,1024]{0,1:T(8,128)(2,1)S(1)}, bf16[16,1024]{0,1:T(8,128)(2,1)}, u32[]{:S(2)}, u32[]{:S(2)}) collective-permute-start(bf16[16,1024]{0,1:T(8,128)(2,1)S(1)} %convert_element_type.162), channel_id=1, source_target_pairs={{0,63},{1,0},{2,1},{3,2},{4,3},{5,4},{6,5},{7,6},{8,7},{9,8},{10,9... | collective-permute-start | bytes 98312 | tf_op jit(solution)/shard_map/ppermute | solution.py:17
  154.0 1.0 copy.241
  155.0 0.7 copy-done.28
  155.7 0.7 copy-done.29
  156.4 6.4 %collective-permute-done.6 = bf16[16,1024]{0,1:T(8,128)(2,1)} collective-permute-done((bf16[16,1024]{0,1:T(8,128)(2,1)S(1)}, bf16[16,1024]{0,1:T(8,128)(2,1)}, u32[]{:S(2)}, u32[]{:S(2)}) %collective-permute-start.6) | collective-permute-done | bytes 32800 | tf_op jit(solution)/shard_map/ppermute | solution.py:17
  162.9 1.4 add_bitcast_fusion
  164.3 0.8 copy.242
  (116 shorter events, 9.2 us)
Async XLA Ops:
  7.2 9.2 %copy-start.10 = (bf16[1,1,256,2048]{3,2,1,0:T(8,128)(2,1)S(1)}, bf16[1,1,256,2048]{3,2,1,0:T(8,128)(2,1)}, u32[]{:S(2)}) copy-start(bf16[1,1,256,2048]{3,2,1,0:T(8,128)(2,1)} %param.6) | copy-start | bytes 3145732
  8.7 17.3 %all-to-all-start = ((bf16[8,16,1024]{2,1,0:T(8,128)(2,1)}), bf16[8,16,1024]{2,1,0:T(8,128)(2,1)}, u32[]{:S(2)}, u32[]{:S(2)}) async-start(bf16[8,16,1024]{2,1,0:T(8,128)(2,1)} %stack.3), calls=%async_computation | async-start | bytes 524288 | tf_op jit(solution)/shard_map/all_to_all | solution.py:31
  15.6 106.4 %reduce-scatter.4.cloned.1.call-start = ((), (), s32[]{:S(2)}) async-start(), calls=%async_computation.2 | async-start | bytes 589824
  16.9 1.4 copy-start.11
  18.3 2.8 %copy-start.3 = (bf16[256,512]{0,1:T(8,128)(2,1)}, bf16[256,512]{0,1:T(8,128)(2,1)S(1)}, u32[]{:S(2)}) copy-start(bf16[256,512]{0,1:T(8,128)(2,1)S(1)} %get-tuple-element.12) | copy-start | bytes 786436
  21.2 12.4 %copy-start.30 = (s32[64]{0:T(128)S(1)}, s32[64]{0:T(128)}, u32[]{:S(2)}) copy-start(s32[64]{0:T(128)} %param.10) | copy-start | bytes 772
  26.0 24.9 %collective-permute-start.5 = (bf16[128,1024]{1,0:T(8,128)(2,1)}, bf16[128,1024]{1,0:T(8,128)(2,1)}, u32[]{:S(2)}, u32[]{:S(2)}) collective-permute-start(bf16[128,1024]{1,0:T(8,128)(2,1)} %bitcast.2), channel_id=1, source_target_pairs={{0,1},{1,2},{2,3},{3,4},{4,5},{5,6},{6,7},{7,8},{8,9},{9,10},{10,1... | collective-permute-start | bytes 786440 | tf_op jit(solution)/shard_map/ppermute | solution.py:17
  36.8 21.5 %collective-permute-start.4 = (bf16[128,1024]{1,0:T(8,128)(2,1)}, bf16[128,1024]{1,0:T(8,128)(2,1)}, u32[]{:S(2)}, u32[]{:S(2)}) collective-permute-start(bf16[128,1024]{1,0:T(8,128)(2,1)} %bitcast.2), channel_id=1, source_target_pairs={{0,63},{1,0},{2,1},{3,2},{4,3},{5,4},{6,5},{7,6},{8,7},{9,8},{10,9... | collective-permute-start | bytes 786440 | tf_op jit(solution)/shard_map/ppermute | solution.py:17
  38.7 19.6 %collective-permute-start.3 = (bf16[128,1024]{1,0:T(8,128)(2,1)}, bf16[128,1024]{1,0:T(8,128)(2,1)}, u32[]{:S(2)}, u32[]{:S(2)}) collective-permute-start(bf16[128,1024]{1,0:T(8,128)(2,1)} %bitcast.2), channel_id=1, source_target_pairs={{0,2},{1,3},{2,4},{3,5},{4,6},{5,7},{6,8},{7,9},{8,10},{9,11},{10,... | collective-permute-start | bytes 786440 | tf_op jit(solution)/shard_map/ppermute | solution.py:17
  41.8 16.5 %collective-permute-start.2 = (bf16[128,1024]{1,0:T(8,128)(2,1)}, bf16[128,1024]{1,0:T(8,128)(2,1)}, u32[]{:S(2)}, u32[]{:S(2)}) collective-permute-start(bf16[128,1024]{1,0:T(8,128)(2,1)} %bitcast.2), channel_id=1, source_target_pairs={{0,62},{1,63},{2,0},{3,1},{4,2},{5,3},{6,4},{7,5},{8,6},{9,7},{10,... | collective-permute-start | bytes 786440 | tf_op jit(solution)/shard_map/ppermute | solution.py:17
  44.0 14.3 %collective-permute-start.1 = (bf16[128,1024]{1,0:T(8,128)(2,1)}, bf16[128,1024]{1,0:T(8,128)(2,1)}, u32[]{:S(2)}, u32[]{:S(2)}) collective-permute-start(bf16[128,1024]{1,0:T(8,128)(2,1)} %bitcast.2), channel_id=1, source_target_pairs={{0,3},{1,4},{2,5},{3,6},{4,7},{5,8},{6,9},{7,10},{8,11},{9,12},{10... | collective-permute-start | bytes 786440 | tf_op jit(solution)/shard_map/ppermute | solution.py:17
  51.0 14.3 %collective-permute-start = (bf16[128,1024]{1,0:T(8,128)(2,1)}, bf16[128,1024]{1,0:T(8,128)(2,1)}, u32[]{:S(2)}, u32[]{:S(2)}) collective-permute-start(bf16[128,1024]{1,0:T(8,128)(2,1)} %bitcast.2), channel_id=1, source_target_pairs={{0,61},{1,62},{2,63},{3,0},{4,1},{5,2},{6,3},{7,4},{8,5},{9,6},{10... | collective-permute-start | bytes 786440 | tf_op jit(solution)/shard_map/ppermute | solution.py:17
  58.3 8.2 %copy-start.4 = (bf16[256,512]{0,1:T(8,128)(2,1)S(1)}, bf16[256,512]{0,1:T(8,128)(2,1)}, u32[]{:S(2)}) copy-start(bf16[256,512]{0,1:T(8,128)(2,1)} %copy-done.3) | copy-start | bytes 786436
  66.3 1.0 copy-start
  66.3 1.2 copy-start.2
  67.9 1.0 copy-start.9
  68.0 1.2 copy-start.15
  68.9 0.8 copy-start.5
  70.1 7.6 %copy-start.7 = (bf16[4,256,256]{1,2,0:T(8,128)(2,1)}, bf16[4,256,256]{1,2,0:T(8,128)(2,1)S(1)}, u32[]{:S(2)}) copy-start(bf16[4,256,256]{1,2,0:T(8,128)(2,1)S(1)} %fusion.16) | copy-start | bytes 1572868
  70.6 1.0 copy-start.21
  73.9 1.0 copy-start.17
  75.9 1.0 copy-start.19
  90.2 2.1 %copy-start.1 = (bf16[256,512]{0,1:T(8,128)(2,1)S(1)}, bf16[256,512]{0,1:T(8,128)(2,1)}, u32[]{:S(2)}) copy-start(bf16[256,512]{0,1:T(8,128)(2,1)} %get-tuple-element.14) | copy-start | bytes 786436
  92.3 2.9 %copy-start.12 = (bf16[256,4,128]{0,2,1:T(8,128)(2,1)S(1)}, bf16[256,4,128]{0,2,1:T(8,128)(2,1)}, u32[]{:S(2)}) copy-start(bf16[256,4,128]{0,2,1:T(8,128)(2,1)} %fusion.50) | copy-start | bytes 786436
  92.4 4.6 %copy-start.13 = (bf16[256,4,128]{0,2,1:T(8,128)(2,1)S(1)}, bf16[256,4,128]{0,2,1:T(8,128)(2,1)}, u32[]{:S(2)}) copy-start(bf16[256,4,128]{0,2,1:T(8,128)(2,1)} %fusion.48) | copy-start | bytes 786436
  93.3 2.8 %copy-start.14 = (bf16[256,4,128]{0,2,1:T(8,128)(2,1)S(1)}, bf16[256,4,128]{0,2,1:T(8,128)(2,1)}, u32[]{:S(2)}) copy-start(bf16[256,4,128]{0,2,1:T(8,128)(2,1)} %fusion.46) | copy-start | bytes 786436
  93.3 4.5 %copy-start.8 = (bf16[4,256,256]{1,2,0:T(8,128)(2,1)S(1)}, bf16[4,256,256]{1,2,0:T(8,128)(2,1)}, u32[]{:S(2)}) copy-start(bf16[4,256,256]{1,2,0:T(8,128)(2,1)} %copy-done.7) | copy-start | bytes 1572868
  96.1 2.7 %copy-start.22 = (bf16[256,512]{0,1:T(8,128)(2,1)S(1)}, bf16[256,512]{0,1:T(8,128)(2,1)}, u32[]{:S(2)}) copy-start(bf16[256,512]{0,1:T(8,128)(2,1)} %get-tuple-element.16) | copy-start | bytes 786436
  96.9 2.8 %copy-start.20 = (bf16[256,512]{0,1:T(8,128)(2,1)S(1)}, bf16[256,512]{0,1:T(8,128)(2,1)}, u32[]{:S(2)}) copy-start(bf16[256,512]{0,1:T(8,128)(2,1)} %get-tuple-element.19) | copy-start | bytes 786436
  98.7 1.9 %copy-start.23 = (bf16[256,512]{1,0:T(8,128)(2,1)S(1)}, bf16[256,512]{1,0:T(8,128)(2,1)}, u32[]{:S(2)}) copy-start(bf16[256,512]{1,0:T(8,128)(2,1)} %copy.224) | copy-start | bytes 786436
  98.7 1.9 %copy-start.24 = (bf16[256,512]{1,0:T(8,128)(2,1)S(1)}, bf16[256,512]{1,0:T(8,128)(2,1)}, u32[]{:S(2)}) copy-start(bf16[256,512]{1,0:T(8,128)(2,1)} %copy.221) | copy-start | bytes 786436
  98.7 1.9 %copy-start.25 = (bf16[256,512]{1,0:T(8,128)(2,1)S(1)}, bf16[256,512]{1,0:T(8,128)(2,1)}, u32[]{:S(2)}) copy-start(bf16[256,512]{1,0:T(8,128)(2,1)} %copy.223) | copy-start | bytes 786436
  98.7 1.9 %copy-start.26 = (bf16[256,512]{1,0:T(8,128)(2,1)S(1)}, bf16[256,512]{1,0:T(8,128)(2,1)}, u32[]{:S(2)}) copy-start(bf16[256,512]{1,0:T(8,128)(2,1)} %copy.222) | copy-start | bytes 786436
  100.6 33.3 %copy-start.27 = (bf16[1,1,256,1024]{2,3,1,0:T(8,128)(2,1)S(1)}, bf16[1,1,256,1024]{2,3,1,0:T(8,128)(2,1)}, u32[]{:S(2)}) copy-start(bf16[1,1,256,1024]{2,3,1,0:T(8,128)(2,1)} %fusion.85) | copy-start | bytes 1572868
  101.8 32.2 %copy-start.18 = (bf16[256,512]{0,1:T(8,128)(2,1)S(1)}, bf16[256,512]{0,1:T(8,128)(2,1)}, u32[]{:S(2)}) copy-start(bf16[256,512]{0,1:T(8,128)(2,1)} %get-tuple-element.18) | copy-start | bytes 786436
  101.8 51.9 %copy-start.6 = (bf16[4,256,256]{1,2,0:T(8,128)(2,1)S(1)}, bf16[4,256,256]{1,2,0:T(8,128)(2,1)}, u32[]{:S(2)}) copy-start(bf16[4,256,256]{1,2,0:T(8,128)(2,1)} %copy-done.5) | copy-start | bytes 1572868
  101.8 51.9 %copy-start.16 = (bf16[256,512]{0,1:T(8,128)(2,1)S(1)}, bf16[256,512]{0,1:T(8,128)(2,1)}, u32[]{:S(2)}) copy-start(bf16[256,512]{0,1:T(8,128)(2,1)} %get-tuple-element.17) | copy-start | bytes 786436
  123.0 28.7 %collective-permute-start.11 = (bf16[16,1024]{0,1:T(8,128)(2,1)S(1)}, bf16[16,1024]{0,1:T(8,128)(2,1)S(1)}, u32[]{:S(2)}, u32[]{:S(2)}) collective-permute-start(bf16[16,1024]{0,1:T(8,128)(2,1)S(1)} %convert_element_type.162), channel_id=1, source_target_pairs={{0,3},{1,4},{2,5},{3,6},{4,7},{5,8},{6,9},{7,10},{8,11},{9,12},{10... | collective-permute-start | bytes 98312 | tf_op jit(solution)/shard_map/ppermute | solution.py:17
  134.3 20.7 %collective-permute-start.10 = (bf16[16,1024]{0,1:T(8,128)(2,1)S(1)}, bf16[16,1024]{0,1:T(8,128)(2,1)S(1)}, u32[]{:S(2)}, u32[]{:S(2)}) collective-permute-start(bf16[16,1024]{0,1:T(8,128)(2,1)S(1)} %convert_element_type.162), channel_id=1, source_target_pairs={{0,61},{1,62},{2,63},{3,0},{4,1},{5,2},{6,3},{7,4},{8,5},{9,6},{10... | collective-permute-start | bytes 98312 | tf_op jit(solution)/shard_map/ppermute | solution.py:17
  136.2 18.8 %collective-permute-start.9 = (bf16[16,1024]{0,1:T(8,128)(2,1)S(1)}, bf16[16,1024]{0,1:T(8,128)(2,1)S(1)}, u32[]{:S(2)}, u32[]{:S(2)}) collective-permute-start(bf16[16,1024]{0,1:T(8,128)(2,1)S(1)} %convert_element_type.162), channel_id=1, source_target_pairs={{0,2},{1,3},{2,4},{3,5},{4,6},{5,7},{6,8},{7,9},{8,10},{9,11},{10,... | collective-permute-start | bytes 98312 | tf_op jit(solution)/shard_map/ppermute | solution.py:17
  139.9 15.1 %collective-permute-start.8 = (bf16[16,1024]{0,1:T(8,128)(2,1)S(1)}, bf16[16,1024]{0,1:T(8,128)(2,1)S(1)}, u32[]{:S(2)}, u32[]{:S(2)}) collective-permute-start(bf16[16,1024]{0,1:T(8,128)(2,1)S(1)} %convert_element_type.162), channel_id=1, source_target_pairs={{0,62},{1,63},{2,0},{3,1},{4,2},{5,3},{6,4},{7,5},{8,6},{9,7},{10,... | collective-permute-start | bytes 98312 | tf_op jit(solution)/shard_map/ppermute | solution.py:17
  141.9 13.2 %collective-permute-start.7 = (bf16[16,1024]{0,1:T(8,128)(2,1)S(1)}, bf16[16,1024]{0,1:T(8,128)(2,1)S(1)}, u32[]{:S(2)}, u32[]{:S(2)}) collective-permute-start(bf16[16,1024]{0,1:T(8,128)(2,1)S(1)} %convert_element_type.162), channel_id=1, source_target_pairs={{0,1},{1,2},{2,3},{3,4},{4,5},{5,6},{6,7},{7,8},{8,9},{9,10},{10,1... | collective-permute-start | bytes 98312 | tf_op jit(solution)/shard_map/ppermute | solution.py:17
  151.8 11.1 %collective-permute-start.6 = (bf16[16,1024]{0,1:T(8,128)(2,1)S(1)}, bf16[16,1024]{0,1:T(8,128)(2,1)}, u32[]{:S(2)}, u32[]{:S(2)}) collective-permute-start(bf16[16,1024]{0,1:T(8,128)(2,1)S(1)} %convert_element_type.162), channel_id=1, source_target_pairs={{0,63},{1,0},{2,1},{3,2},{4,3},{5,4},{6,5},{7,6},{8,7},{9,8},{10,9... | collective-permute-start | bytes 98312 | tf_op jit(solution)/shard_map/ppermute | solution.py:17
  155.0 0.7 copy-start.28
  155.7 0.7 copy-start.29
Sparse Core Ops, SparseCore 0:
  92.5 29.4 reduce-scatter.3
